TPU v7x, 256 devices: a whole 4x4x8 slice. The times are simulated.
256 devices in a mesh: seq: 8 (over y, core), dp: 32 (over z, x).
Axes of the slice: x: 4, y: 4, z: 8, core: 2. Of those that a mesh axis runs over, the one named last changes fastest.
Arguments:
- q_rows: bfloat16 [32768, 2048], P(('seq', 'dp')), may hold values from -6 to 6
- key_rows: bfloat16 [32768, 512], P(('seq', 'dp')), may hold values from -6 to 6
- value_rows: bfloat16 [32768, 512], P(('seq', 'dp')), may hold values from -6 to 6
- pack_peer: int32 [4096], P(('seq', 'dp')), may hold values from 0 to 31, as said below
- pack_slot: int32 [4096], P(('seq', 'dp')), may hold values from 0 to 15
- doc_ids: int32 [32, 1024], P('dp'), may hold values from 0 to 7, never falling along the last dimension, each value on 1 to 512 neighbouring positions
- grad_out: bfloat16 [32, 1024, 2048], P('dp', 'seq'), may hold values from -6 to 6
- out_weight: bfloat16 [2048, 2048], P(('seq', 'dp')), may hold values from -0.125 to 0.125
Outputs:
- dq_rows: bfloat16 [32768, 2048], P(('seq', 'dp'))
- key_gradient_rows: bfloat16 [32768, 512], P(('seq', 'dp'))
- value_gradient_rows: bfloat16 [32768, 512], P(('seq', 'dp'))
- wo_grad: float32 [2048, 2048], P(('seq', 'dp'))
Inputs may be any that keep to these rules, and one draw needn't show every extreme that they name: `pack_peer`: blocks keep their seq index; every block position of every packed sequence receives exactly one block; the 16 blocks of one device send at most 1 block to one packed sequence, and exactly 1 to some.
All inputs are finite; a program needn't handle non-finite values.
Results may differ from a plain program's by a relative error of at most 0.03.
Values may be sent and summed in bfloat16 or wider, within the bound.
A program may use at most 64 MiB of HBM per device.

v0:
```python
import math
import jax
import jax.numpy as jnp
from jax import lax
from jax.sharding import PartitionSpec as P

HEAD_SIZE = 128
PACK = 8
QBLK = 512
NEG_FILL = -1e30


def body(q_rows, key_rows, value_rows, pack_peer, pack_slot, doc_ids, grad_out, out_weight):
    seq_count = lax.axis_size("seq")
    dp_count = lax.axis_size("dp")
    tok_dev = q_rows.shape[0]
    kv_heads = key_rows.shape[1] // HEAD_SIZE
    block_count = pack_peer.shape[0]
    capacity = (block_count + dp_count - 1) // dp_count
    soft_scale = 1.0 / math.sqrt(HEAD_SIZE)
    grad_scale = 8.0 / math.sqrt(dp_count * seq_count * tok_dev)
    same_peer = pack_peer[:, None] == pack_peer[None, :]
    earlier = lax.broadcasted_iota(jnp.int32, (block_count, block_count), 1) < lax.broadcasted_iota(
        jnp.int32, (block_count, block_count), 0
    )
    peer_rank = jnp.sum((same_peer & earlier).astype(jnp.int32), axis=1)
    send_index = pack_peer * capacity + peer_rank

    def to_slots(sample_rows):
        columns = sample_rows.shape[1]
        head_grouped = sample_rows.reshape(block_count, PACK, columns)
        blank = jnp.zeros((dp_count * capacity, PACK, columns), sample_rows.dtype)
        return blank.at[send_index].set(head_grouped)

    slot_tag = (
        jnp.full((dp_count * capacity,), block_count, jnp.int32).at[send_index].set(pack_slot)
    )
    slot_tag = slot_tag.astype(jnp.bfloat16).reshape(dp_count, capacity)
    came_q, came_k, came_v, came_tag = (
        lax.all_to_all(to_slots(q_rows), "dp", split_axis=0, concat_axis=0, tiled=True),
        lax.all_to_all(to_slots(key_rows), "dp", split_axis=0, concat_axis=0, tiled=True),
        lax.all_to_all(to_slots(value_rows), "dp", split_axis=0, concat_axis=0, tiled=True),
        lax.all_to_all(slot_tag, "dp", split_axis=0, concat_axis=0, tiled=True),
    )
    landing = came_tag.reshape(-1).astype(jnp.int32)

    def from_slots(arrived):
        columns = arrived.shape[2]
        blank = jnp.zeros((block_count, PACK, columns), arrived.dtype)
        return blank.at[landing].set(arrived, mode="drop").reshape(tok_dev, columns)

    packed_q = from_slots(came_q)
    packed_keys = from_slots(came_k)
    packed_values = from_slots(came_v)
    repeat_count = seq_count // kv_heads

    def widen(packed_rows):
        split_heads = packed_rows.reshape(tok_dev, kv_heads, HEAD_SIZE)
        return jnp.repeat(split_heads, repeat_count, axis=1).reshape(tok_dev, seq_count * HEAD_SIZE)

    head_q, head_k, head_v = (
        lax.all_to_all(packed_q, "seq", split_axis=1, concat_axis=0, tiled=True),
        lax.all_to_all(widen(packed_keys), "seq", split_axis=1, concat_axis=0, tiled=True),
        lax.all_to_all(widen(packed_values), "seq", split_axis=1, concat_axis=0, tiled=True),
    )
    seq_len = head_q.shape[0]
    head_group = head_q.shape[1] // HEAD_SIZE
    query_blocks = seq_len // QBLK
    doc_full = doc_ids[0]
    firsts = doc_full.reshape(query_blocks, QBLK)[:, 0]
    key_starts = jnp.sum((doc_full[None, :] < firsts[:, None]).astype(jnp.int32), axis=1) // QBLK
    q_blocks = head_q.reshape(query_blocks, QBLK, head_group, HEAD_SIZE)
    local_pos = lax.broadcasted_iota(jnp.int32, (QBLK,), 0)

    def block_scores(q_block, q_index, k_index):
        k_block = lax.dynamic_slice_in_dim(head_k, k_index * QBLK, QBLK, 0)
        raw = (
            jnp.einsum("qgd,kd->gqk", q_block, k_block, preferred_element_type=jnp.float32)
            * soft_scale
        )
        q_docs = lax.dynamic_slice_in_dim(doc_full, q_index * QBLK, QBLK, 0)
        k_docs = lax.dynamic_slice_in_dim(doc_full, k_index * QBLK, QBLK, 0)
        q_pos = q_index * QBLK + local_pos
        k_pos = k_index * QBLK + local_pos
        allowed = (q_docs[:, None] == k_docs[None, :]) & (q_pos[:, None] >= k_pos[None, :])
        return (jnp.where(allowed[None], raw, NEG_FILL), allowed, k_block)

    def lse_block(q_index):
        q_block = q_blocks[q_index]

        def lse_advance(k_index, state):
            running_top, running_total = state
            masked, allowed, k_block = block_scores(q_block, q_index, k_index)
            new_top = jnp.maximum(running_top, jnp.max(masked, axis=2))
            terms = jnp.where(allowed[None], jnp.exp(masked - new_top[:, :, None]), 0.0)
            running_total = running_total * jnp.exp(running_top - new_top) + jnp.sum(terms, axis=2)
            return (new_top, running_total)

        start_state = (
            jnp.full((head_group, QBLK), NEG_FILL, jnp.float32),
            jnp.zeros((head_group, QBLK), jnp.float32),
        )
        final_top, final_total = lax.fori_loop(
            key_starts[q_index], q_index + 1, lse_advance, start_state
        )
        return final_top + jnp.log(final_total)

    block_ids = jnp.arange(query_blocks, dtype=jnp.int32)
    log_totals = lax.map(lse_block, block_ids)

    def output_block(q_index):
        q_block = q_blocks[q_index]
        row_lse = log_totals[q_index]

        def output_advance(k_index, summed):
            masked, allowed, k_block = block_scores(q_block, q_index, k_index)
            v_block = lax.dynamic_slice_in_dim(head_v, k_index * QBLK, QBLK, 0)
            weights_low = jnp.where(
                allowed[None], jnp.exp(masked - row_lse[:, :, None]), 0.0
            ).astype(jnp.bfloat16)
            return summed + jnp.einsum(
                "gqk,kd->gqd", weights_low, v_block, preferred_element_type=jnp.float32
            )

        summed = lax.fori_loop(
            key_starts[q_index],
            q_index + 1,
            output_advance,
            jnp.zeros((head_group, QBLK, HEAD_SIZE), jnp.float32),
        )
        return jnp.transpose(summed.astype(jnp.bfloat16), (1, 0, 2)).reshape(
            QBLK, head_group * HEAD_SIZE
        )

    head_out = lax.map(output_block, block_ids).reshape(seq_len, head_group * HEAD_SIZE)
    grad_tok = grad_out[0]
    tok_out = lax.all_to_all(head_out, "seq", split_axis=0, concat_axis=1, tiled=True)
    tok_grad = lax.dot_general(
        grad_tok,
        lax.all_gather(out_weight, ("seq", "dp"), axis=0, tiled=True),
        (((1,), (1,)), ((), ())),
        preferred_element_type=jnp.float32,
    ).astype(jnp.bfloat16)
    columns = tok_out
    seq_part = lax.psum_scatter(
        lax.dot_general(
            columns, grad_tok, (((0,), (0,)), ((), ())), preferred_element_type=jnp.float32
        ).astype(jnp.bfloat16),
        "seq",
        scatter_dimension=0,
        tiled=True,
    )
    head_grad = lax.all_to_all(tok_grad, "seq", split_axis=1, concat_axis=0, tiled=True)
    weight_grad = (
        lax.psum_scatter(seq_part, "dp", scatter_dimension=0, tiled=True).astype(jnp.float32)
        * grad_scale
    )
    grad_blocks = head_grad.reshape(query_blocks, QBLK, head_group, HEAD_SIZE)
    out_blocks = head_out.reshape(query_blocks, QBLK, head_group, HEAD_SIZE)

    def backward_block(state, q_index):
        key_sum, value_sum = state
        q_block = q_blocks[q_index]
        g_block = grad_blocks[q_index]
        row_lse = log_totals[q_index]
        delta = jnp.einsum(
            "qgd,qgd->gq", g_block, out_blocks[q_index], preferred_element_type=jnp.float32
        )

        def backward_advance(k_index, inner):
            query_sum, key_sum, value_sum = inner
            masked, allowed, k_block = block_scores(q_block, q_index, k_index)
            v_block = lax.dynamic_slice_in_dim(head_v, k_index * QBLK, QBLK, 0)
            weights = jnp.where(allowed[None], jnp.exp(masked - row_lse[:, :, None]), 0.0)
            dweights = jnp.einsum(
                "qgd,kd->gqk", g_block, v_block, preferred_element_type=jnp.float32
            )
            dscores = (weights * (dweights - delta[:, :, None])).astype(jnp.bfloat16)
            query_sum = query_sum + jnp.einsum(
                "gqk,kd->gqd", dscores, k_block, preferred_element_type=jnp.float32
            )
            key_piece = jnp.einsum(
                "gqk,qgd->kd", dscores, q_block, preferred_element_type=jnp.float32
            )
            value_piece = jnp.einsum(
                "gqk,qgd->kd",
                weights.astype(jnp.bfloat16),
                g_block,
                preferred_element_type=jnp.float32,
            )
            key_old = lax.dynamic_slice_in_dim(key_sum, k_index * QBLK, QBLK, 0)
            value_old = lax.dynamic_slice_in_dim(value_sum, k_index * QBLK, QBLK, 0)
            key_sum = lax.dynamic_update_slice_in_dim(
                key_sum, key_old + key_piece, k_index * QBLK, 0
            )
            value_sum = lax.dynamic_update_slice_in_dim(
                value_sum, value_old + value_piece, k_index * QBLK, 0
            )
            return (query_sum, key_sum, value_sum)

        start_inner = (jnp.zeros((head_group, QBLK, HEAD_SIZE), jnp.float32), key_sum, value_sum)
        query_sum, key_sum, value_sum = lax.fori_loop(
            key_starts[q_index], q_index + 1, backward_advance, start_inner
        )
        dq_block = jnp.transpose((query_sum * soft_scale).astype(jnp.bfloat16), (1, 0, 2)).reshape(
            QBLK, head_group * HEAD_SIZE
        )
        return ((key_sum, value_sum), dq_block)

    start_sums = (
        jnp.zeros((seq_len, HEAD_SIZE), jnp.float32),
        jnp.zeros((seq_len, HEAD_SIZE), jnp.float32),
    )
    (key_sum, value_sum), dq_blocks = lax.scan(backward_block, start_sums, block_ids)
    head_dq = dq_blocks.reshape(seq_len, head_group * HEAD_SIZE)
    key_part = (key_sum * soft_scale).astype(jnp.bfloat16)
    value_part = value_sum.astype(jnp.bfloat16)
    back_q, back_k, back_v = (
        lax.all_to_all(head_dq, "seq", split_axis=0, concat_axis=1, tiled=True),
        lax.all_to_all(key_part, "seq", split_axis=0, concat_axis=1, tiled=True),
        lax.all_to_all(value_part, "seq", split_axis=0, concat_axis=1, tiled=True),
    )

    def merge_groups(back_rows):
        split_groups = back_rows.reshape(tok_dev, kv_heads, repeat_count, HEAD_SIZE).astype(
            jnp.float32
        )
        return (
            jnp.sum(split_groups, axis=2)
            .astype(jnp.bfloat16)
            .reshape(tok_dev, kv_heads * HEAD_SIZE)
        )

    dk_tok = merge_groups(back_k)
    dv_tok = merge_groups(back_v)

    def to_sources(packed_rows):
        columns = packed_rows.shape[1]
        head_grouped = packed_rows.reshape(block_count, PACK, columns)
        picked = jnp.take(head_grouped, jnp.minimum(landing, block_count - 1), axis=0)
        return picked

    ret_q, ret_k, ret_v = (
        lax.all_to_all(to_sources(back_q), "dp", split_axis=0, concat_axis=0, tiled=True),
        lax.all_to_all(to_sources(dk_tok), "dp", split_axis=0, concat_axis=0, tiled=True),
        lax.all_to_all(to_sources(dv_tok), "dp", split_axis=0, concat_axis=0, tiled=True),
    )

    def to_samples(returned):
        columns = returned.shape[2]
        return jnp.take(returned, send_index, axis=0).reshape(tok_dev, columns)

    return (to_samples(ret_q), to_samples(ret_k), to_samples(ret_v), weight_grad)


def solution(mesh):
    return jax.shard_map(
        body,
        mesh=mesh,
        in_specs=(
            P(("seq", "dp"), None),
            P(("seq", "dp"), None),
            P(("seq", "dp"), None),
            P(("seq", "dp")),
            P(("seq", "dp")),
            P("dp", None),
            P("dp", "seq", None),
            P(("seq", "dp"), None),
        ),
        out_specs=(
            P(("seq", "dp"), None),
            P(("seq", "dp"), None),
            P(("seq", "dp"), None),
            P(("seq", "dp"), None),
        ),
        check_vma=False,
    )
```

profile of v0, /device:TPU:8, one launch (start us, length us, event | category | flops | bytes accessed | tf_op | source)
XLA Modules:
  0.0 582.6 jit_solution(11790713067474264996)
XLA Ops:
  11.6 11.3 %all-to-all-start = ((bf16[32,1,1]{2,1,0:T(2,128)(2,1)}), bf16[32,1,1]{2,1,0:T(2,128)(2,1)S(1)}, u32[]{:S(2)}, u32[]{:S(2)}) async-start(bf16[32,1,1]{2,1,0:T(2,128)(2,1)} %copy.81), calls=%async_computation | async-start | bytes 32768 | tf_op jit(solution)/shard_map/all_to_all | solution.py:43
  26.1 6.5 %all-to-all-done = bf16[32,1,1]{2,1,0:T(2,128)(2,1)S(1)} async-done(((bf16[32,1,1]{2,1,0:T(2,128)(2,1)}), bf16[32,1,1]{2,1,0:T(2,128)(2,1)S(1)}, u32[]{:S(2)}, u32[]{:S(2)}) %all-to-all-start) | async-done | bytes 96 | tf_op jit(solution)/shard_map/all_to_all | solution.py:43
  40.2 8.3 %all-to-all-done.3 = bf16[32,8,512]{2,1,0:T(8,128)(2,1)S(1)} async-done(((bf16[32,8,512]{2,1,0:T(8,128)(2,1)}), bf16[32,8,512]{2,1,0:T(8,128)(2,1)S(1)}, u32[]{:S(2)}, u32[]{:S(2)}) %all-to-all-start.3) | async-done | bytes 262176 | tf_op jit(solution)/shard_map/all_to_all | solution.py:41
  55.4 22.5 %all-to-all-done.1 = bf16[32,8,2048]{2,1,0:T(8,128)(2,1)S(1)} async-done(((bf16[32,8,2048]{2,1,0:T(8,128)(2,1)}), bf16[32,8,2048]{2,1,0:T(8,128)(2,1)S(1)}, u32[]{:S(2)}, u32[]{:S(2)}) %all-to-all-start.1) | async-done | bytes 1048608 | tf_op jit(solution)/shard_map/all_to_all | solution.py:40
  77.9 5.4 all-to-all-start.6
  87.8 7.0 %all-to-all-done.6 = bf16[32,8,512]{2,1,0:T(8,128)(2,1)S(1)} async-done(((bf16[32,8,512]{2,1,0:T(8,128)(2,1)}), bf16[32,8,512]{2,1,0:T(8,128)(2,1)S(1)}, u32[]{:S(2)}, u32[]{:S(2)}) %all-to-all-start.6) | async-done | bytes 262176 | tf_op jit(solution)/shard_map/all_to_all | solution.py:42
  125.7 23.2 %while.92 = (s32[]{:T(128)}, f32[2,2,512]{2,1,0:T(2,128)S(1)}, s32[2]{0:T(128)S(1)}, s32[2]{0:T(128)S(1)}, bf16[2,512,2,128]{3,1,2,0:T(8,128)(2,1)}, /*index=5*/...) while((s32[]{:T(128)}, f32[2,2,512]{2,1,0:T(2,128)S(1)}, ...), condition=%wide.region_12.13_spmd.clone.clone, body=%wide.region_7.12_spmd.clone.clone.sunk | while | flops 139202576 | bytes 5997168 | solution.py:109
  140.4 8.5 %while.97 = (s32[]{:T(128)}, f32[2,512]{1,0:T(2,128)S(1)}, f32[2,512]{1,0:T(2,128)S(1)}, s32[]{:T(128)}, s32[512]{0:T(512)S(1)}, /*index=5*/s32[1024]{0:T(1024)S...) while((s32[]{:T(128)}, f32[2,512]{1,0:T(2,128)S(1)}, ...), condition=%wide.region_11.11_spmd.clone, body=%wide.region_8.10_spmd.clone.sunk | while | flops 139201536 | bytes 5445827 | solution.py:103
  149.8 27.0 %while.94 = (s32[]{:T(128)}, bf16[2,512,256]{2,1,0:T(8,128)(2,1)}, s32[2]{0:T(128)S(1)}, s32[2]{0:T(128)S(1)}, bf16[2,512,2,128]{3,1,2,0:T(8,128)(2,1)}, /*index...) while((s32[]{:T(128)}, bf16[2,512,256]{2,1,0:T(8,128)(2,1)}, ...), condition=%wide.region_18.19_spmd.clone.clone, body=%wide.region_15.18_spmd.clone.clone.sunk | while | flops 272106496 | bytes 5543548 | solution.py:135
  166.8 8.8 %while.98 = (s32[]{:T(128)}, f32[2,512,128]{2,1,0:T(8,128)S(1)}, s32[]{:T(128)}, s32[512]{0:T(512)S(1)}, s32[1024]{0:T(1024)S(1)}, /*index=5*/s32[]{:T(128)}, s3...) while((s32[]{:T(128)}, f32[2,512,128]{2,1,0:T(8,128)S(1)}, ...), condition=%wide.region_17.17_spmd.clone, body=%wide.region_16.16_spmd.clone.sunk | while | flops 271975424 | bytes 2120903 | solution.py:125
  183.7 9.5 %all-to-all-done.14 = bf16[8,128,256]{2,1,0:T(8,128)(2,1)S(1)} async-done(((bf16[8,128,256]{2,1,0:T(8,128)(2,1)}), bf16[8,128,256]{2,1,0:T(8,128)(2,1)S(1)}, u32[]{:S(2)}, u32[]{:S(2)}) %all-to-all-start.14) | async-done | bytes 524320 | tf_op jit(solution)/shard_map/all_to_all | solution.py:137
  193.4 24.4 %all-gather.2.cloned.1.call-done = bf16[2048,2048]{1,0:T(8,128)(2,1)} async-done(((bf16[8,2048]{1,0:T(8,128)(2,1)}), bf16[2048,2048]{1,0:T(8,128)(2,1)}) %all-gather.2.cloned.1.call-update) | async-done | bytes 8388624 | tf_op jit(solution)/shard_map/all_gather | solution.py:140
  217.8 6.3 %convolution_convert_fusion.1 = bf16[128,2048]{1,0:T(8,128)(2,1)S(1)} fusion(bf16[2048,2048]{1,0:T(8,128)(2,1)} %all-gather.2.cloned.1.call-done, bf16[1,128,2048]{2,1,0:T(8,128)(2,1)S(1)} %copy-done), kind=kOutput, calls=%fused_computation.93 | convolution fusion | flops 1074003968 | bytes 9437184 | tf_op jit(solution)/shard_map/dot_general | solution.py:138
  229.7 5.5 convolution_convert_fusion
  240.4 37.3 %while.96 = (s32[]{:T(128)}, f32[1024,128]{1,0:T(8,128)S(1)}, f32[1024,128]{1,0:T(8,128)S(1)}, bf16[2,512,256]{2,1,0:T(8,128)(2,1)}, s32[2]{0:T(128)S(1)}, /*ind...) while((s32[]{:T(128)}, f32[1024,128]{1,0:T(8,128)S(1)}, ...), condition=%wide.region_22.23_spmd.clone.clone, body=%wide.region_19.22_spmd.clone.clone.sunk | while | flops 677117952 | bytes 19321592 | solution.py:214
  248.9 6.2 %while.99 = (s32[]{:T(128)}, f32[2,512,128]{2,1,0:T(8,128)S(1)}, f32[1024,128]{1,0:T(8,128)S(1)}, f32[1024,128]{1,0:T(8,128)S(1)}, s32[]{:T(128)}, /*index=5*/s3...) while((s32[]{:T(128)}, f32[2,512,128]{2,1,0:T(8,128)S(1)}, ...), condition=%wide.region_21.21_spmd.clone, body=%wide.region_20.20_spmd.clone.sunk | while | flops 676332544 | bytes 13527291 | solution.py:202
  264.8 11.7 %while.99 = (s32[]{:T(128)}, f32[2,512,128]{2,1,0:T(8,128)S(1)}, f32[1024,128]{1,0:T(8,128)S(1)}, f32[1024,128]{1,0:T(8,128)S(1)}, s32[]{:T(128)}, /*index=5*/s3...) while((s32[]{:T(128)}, f32[2,512,128]{2,1,0:T(8,128)S(1)}, ...), condition=%wide.region_21.21_spmd.clone, body=%wide.region_20.20_spmd.clone.sunk | while | flops 676332544 | bytes 13527291 | solution.py:202
  284.0 5.4 all-to-all-done.10
  294.1 6.1 %all-to-all-done.12 = bf16[8,128,128]{2,1,0:T(8,128)(2,1)S(1)} async-done(((bf16[8,128,128]{2,1,0:T(8,128)(2,1)}), bf16[8,128,128]{2,1,0:T(8,128)(2,1)S(1)}, u32[]{:S(2)}, u32[]{:S(2)}) %all-to-all-start.12) | async-done | bytes 262176 | tf_op jit(solution)/shard_map/all_to_all | solution.py:221
  307.5 6.5 %all-to-all-done.8 = bf16[8,128,256]{2,1,0:T(8,128)(2,1)S(1)} async-done(((bf16[8,128,256]{2,1,0:T(8,128)(2,1)}), bf16[8,128,256]{2,1,0:T(8,128)(2,1)S(1)}, u32[]{:S(2)}, u32[]{:S(2)}) %all-to-all-start.8) | async-done | bytes 524320 | tf_op jit(solution)/shard_map/all_to_all | solution.py:219
  314.0 20.1 %all_to_all.176 = bf16[32,8,512]{2,1,0:T(8,128)(2,1)S(1)} all-to-all(bf16[32,8,512]{2,1,0:T(8,128)(2,1)S(1)} %get-tuple-element.1148), channel_id=1, replica_groups=mesh['seq'=8,'dp'=32] {'dp'}, dimensions={0} | all-to-all | bytes 524288 | tf_op jit(solution)/shard_map/all_to_all | solution.py:246
  340.5 10.0 %all-to-all-done.11 = bf16[32,8,512]{2,1,0:T(8,128)(2,1)S(1)} async-done(((bf16[32,8,512]{2,1,0:T(8,128)(2,1)}), bf16[32,8,512]{2,1,0:T(8,128)(2,1)S(1)}, u32[]{:S(2)}, u32[]{:S(2)}) %all-to-all-start.11) | async-done | bytes 262176 | tf_op jit(solution)/shard_map/all_to_all | solution.py:245
  357.2 23.5 %all-to-all-done.9 = bf16[32,8,2048]{2,1,0:T(8,128)(2,1)S(1)} async-done(((bf16[32,8,2048]{2,1,0:T(8,128)(2,1)}), bf16[32,8,2048]{2,1,0:T(8,128)(2,1)S(1)}, u32[]{:S(2)}, u32[]{:S(2)}) %all-to-all-start.9) | async-done | bytes 1048608 | tf_op jit(solution)/shard_map/all_to_all | solution.py:244
  382.1 191.6 %reduce-scatter.5.cloned.1.call-done = bf16[8,2048]{1,0:T(8,128)(2,1)} async-done(((bf16[256,2048]{1,0:T(8,128)(2,1)}), bf16[8,2048]{1,0:T(8,128)(2,1)}) %reduce-scatter.5.cloned.1.call-update) | async-done | bytes 32784 | tf_op jit(solution)/shard_map/reduce_scatter | solution.py:155
  (245 shorter events, 161.3 us)
Async XLA Ops:
  8.0 209.8 %copy-start = (bf16[1,128,2048]{2,1,0:T(8,128)(2,1)S(1)}, bf16[1,128,2048]{2,1,0:T(8,128)(2,1)}, u32[]{:S(2)}) copy-start(bf16[1,128,2048]{2,1,0:T(8,128)(2,1)} %param.30) | copy-start | bytes 1572868
  8.0 29.6 %copy-start.2 = (bf16[128,2048]{1,0:T(8,128)(2,1)S(1)}, bf16[128,2048]{1,0:T(8,128)(2,1)}, u32[]{:S(2)}) copy-start(bf16[128,2048]{1,0:T(8,128)(2,1)} %param.24) | copy-start | bytes 1572868
  10.1 43.1 %copy-start.4 = (s32[16]{0:T(128)}, s32[16]{0:T(128)S(1)}, u32[]{:S(2)}) copy-start(s32[16]{0:T(128)S(1)} %get-tuple-element.1134) | copy-start | bytes 196
  11.6 21.0 %all-to-all-start = ((bf16[32,1,1]{2,1,0:T(2,128)(2,1)}), bf16[32,1,1]{2,1,0:T(2,128)(2,1)S(1)}, u32[]{:S(2)}, u32[]{:S(2)}) async-start(bf16[32,1,1]{2,1,0:T(2,128)(2,1)} %copy.81), calls=%async_computation | async-start | bytes 32768 | tf_op jit(solution)/shard_map/all_to_all | solution.py:43
  32.6 15.9 %all-to-all-start.3 = ((bf16[32,8,512]{2,1,0:T(8,128)(2,1)}), bf16[32,8,512]{2,1,0:T(8,128)(2,1)S(1)}, u32[]{:S(2)}, u32[]{:S(2)}) async-start(bf16[32,8,512]{2,1,0:T(8,128)(2,1)} %scatter_fusion.2), calls=%async_computation.3 | async-start | bytes 524288 | tf_op jit(solution)/shard_map/all_to_all | solution.py:41
  37.6 15.6 %copy-start.3 = (bf16[128,512]{1,0:T(8,128)(2,1)S(1)}, bf16[128,512]{1,0:T(8,128)(2,1)}, u32[]{:S(2)}) copy-start(bf16[128,512]{1,0:T(8,128)(2,1)} %param.26) | copy-start | bytes 393220
  48.5 29.4 %all-to-all-start.1 = ((bf16[32,8,2048]{2,1,0:T(8,128)(2,1)}), bf16[32,8,2048]{2,1,0:T(8,128)(2,1)S(1)}, u32[]{:S(2)}, u32[]{:S(2)}) async-start(bf16[32,8,2048]{2,1,0:T(8,128)(2,1)} %scatter_fusion), calls=%async_computation.1 | async-start | bytes 2097152 | tf_op jit(solution)/shard_map/all_to_all | solution.py:40
  77.9 16.9 %all-to-all-start.6 = ((bf16[32,8,512]{2,1,0:T(8,128)(2,1)}), bf16[32,8,512]{2,1,0:T(8,128)(2,1)S(1)}, u32[]{:S(2)}, u32[]{:S(2)}) async-start(bf16[32,8,512]{2,1,0:T(8,128)(2,1)} %scatter_fusion.4), calls=%async_computation.6 | async-start | bytes 524288 | tf_op jit(solution)/shard_map/all_to_all | solution.py:42
  94.7 13.8 %all-to-all-start.2 = ((bf16[128,8,256]{2,0,1:T(8,128)(2,1)}), bf16[128,8,256]{2,0,1:T(8,128)(2,1)S(1)}, u32[]{:S(2)}, u32[]{:S(2)}) async-start(bf16[128,8,256]{2,0,1:T(8,128)(2,1)} %copy.83), calls=%async_computation.2 | async-start | bytes 1048576 | tf_op jit(solution)/shard_map/all_to_all | solution.py:62
  99.6 118.1 %all-gather.2.cloned.1.call-start = ((), (), s32[]{:S(2)}) async-start(), calls=%async_computation.17 | async-start | bytes 8421376 | tf_op jit(solution)/shard_map/all_gather | solution.py:140
  109.3 10.9 %all-to-all-start.4 = ((bf16[128,8,128]{2,0,1:T(8,128)(2,1)}), bf16[128,8,128]{2,0,1:T(8,128)(2,1)S(1)}, u32[]{:S(2)}, u32[]{:S(2)}) async-start(bf16[128,8,128]{2,0,1:T(8,128)(2,1)} %bitcast.9), calls=%async_computation.4 | async-start | bytes 524288 | tf_op jit(solution)/shard_map/all_to_all | solution.py:63
  120.9 28.0 %all-to-all-start.7 = ((bf16[128,8,128]{2,0,1:T(8,128)(2,1)}), bf16[128,8,128]{2,0,1:T(8,128)(2,1)S(1)}, u32[]{:S(2)}, u32[]{:S(2)}) async-start(bf16[128,8,128]{2,0,1:T(8,128)(2,1)} %bitcast.16), calls=%async_computation.7 | async-start | bytes 524288 | tf_op jit(solution)/shard_map/all_to_all | solution.py:64
  176.8 16.3 %all-to-all-start.14 = ((bf16[8,128,256]{2,1,0:T(8,128)(2,1)}), bf16[8,128,256]{2,1,0:T(8,128)(2,1)S(1)}, u32[]{:S(2)}, u32[]{:S(2)}) async-start(bf16[8,128,256]{2,1,0:T(8,128)(2,1)} %bitcast.31), calls=%async_computation.14 | async-start | bytes 1048576 | tf_op jit(solution)/shard_map/all_to_all | solution.py:137
  224.8 13.7 %all-to-all-start.5 = ((bf16[128,8,256]{2,0,1:T(8,128)(2,1)}), bf16[128,8,256]{2,0,1:T(8,128)(2,1)S(1)}, u32[]{:S(2)}, u32[]{:S(2)}) async-start(bf16[128,8,256]{2,0,1:T(8,128)(2,1)} %bitcast.163), calls=%async_computation.5 | async-start | bytes 1048576 | tf_op jit(solution)/shard_map/all_to_all | solution.py:153
  229.7 124.9 %reduce-scatter.3.cloned.1.call-start = ((), (), s32[]{:S(2)}) async-start(), calls=%async_computation.18 | async-start | bytes 9437184 | tf_op jit(solution)/shard_map/reduce_scatter | solution.py:145
  240.4 42.8 %copy-start.8 = (s32[32]{0:T(128)S(1)}, s32[32]{0:T(128)}, u32[]{:S(2)}) copy-start(s32[32]{0:T(128)} %get-tuple-element.1001) | copy-start | bytes 388
  278.5 10.9 %all-to-all-start.10 = ((bf16[8,128,128]{2,1,0:T(8,128)(2,1)}), bf16[8,128,128]{2,1,0:T(8,128)(2,1)S(1)}, u32[]{:S(2)}, u32[]{:S(2)}) async-start(bf16[8,128,128]{2,1,0:T(8,128)(2,1)} %bitcast.23), calls=%async_computation.10 | async-start | bytes 524288 | tf_op jit(solution)/shard_map/all_to_all | solution.py:220
  289.3 10.9 %all-to-all-start.12 = ((bf16[8,128,128]{2,1,0:T(8,128)(2,1)}), bf16[8,128,128]{2,1,0:T(8,128)(2,1)S(1)}, u32[]{:S(2)}, u32[]{:S(2)}) async-start(bf16[8,128,128]{2,1,0:T(8,128)(2,1)} %bitcast.27), calls=%async_computation.12 | async-start | bytes 524288 | tf_op jit(solution)/shard_map/all_to_all | solution.py:221
  300.2 13.8 %all-to-all-start.8 = ((bf16[8,128,256]{2,1,0:T(8,128)(2,1)}), bf16[8,128,256]{2,1,0:T(8,128)(2,1)S(1)}, u32[]{:S(2)}, u32[]{:S(2)}) async-start(bf16[8,128,256]{2,1,0:T(8,128)(2,1)} %bitcast.19), calls=%async_computation.8 | async-start | bytes 1048576 | tf_op jit(solution)/shard_map/all_to_all | solution.py:219
  305.3 32.9 %copy-start.7 = (s32[32]{0:T(128)S(1)}, s32[32]{0:T(128)}, u32[]{:S(2)}) copy-start(s32[32]{0:T(128)} %get-tuple-element.1150) | copy-start | bytes 388
  334.1 16.4 %all-to-all-start.11 = ((bf16[32,8,512]{2,1,0:T(8,128)(2,1)}), bf16[32,8,512]{2,1,0:T(8,128)(2,1)S(1)}, u32[]{:S(2)}, u32[]{:S(2)}) async-start(bf16[32,8,512]{2,1,0:T(8,128)(2,1)} %get-tuple-element.1149), calls=%async_computation.11 | async-start | bytes 524288 | tf_op jit(solution)/shard_map/all_to_all | solution.py:245
  340.5 14.7 %copy-start.5 = (s32[16]{0:T(128)S(1)}, s32[16]{0:T(128)}, u32[]{:S(2)}) copy-start(s32[16]{0:T(128)} %copy-done.4) | copy-start | bytes 196
  350.5 30.1 %all-to-all-start.9 = ((bf16[32,8,2048]{2,1,0:T(8,128)(2,1)}), bf16[32,8,2048]{2,1,0:T(8,128)(2,1)S(1)}, u32[]{:S(2)}, u32[]{:S(2)}) async-start(bf16[32,8,2048]{2,1,0:T(8,128)(2,1)} %broadcast_select_fusion), calls=%async_computation.9 | async-start | bytes 2097152 | tf_op jit(solution)/shard_map/all_to_all | solution.py:244
  354.5 219.3 %reduce-scatter.5.cloned.1.call-start = ((), (), s32[]{:S(2)}) async-start(), calls=%async_computation.19 | async-start | bytes 1081344 | tf_op jit(solution)/shard_map/reduce_scatter | solution.py:155
  (2 other events, 28.7 us)
Sparse Core Ops, SparseCore 0:
  104.2 113.5 all-gather.1
Sparse Core Ops, SparseCore 1:
  235.3 50.0 reduce-scatter.2
  358.8 214.9 reduce-scatter.4
where the time goes:
time: 585 us; the launch traced here: 583 us
  waiting for transfers between devices  334 us (57%)
  starting transfers between devices  71.1 us (12%)
  local copies, waits for them, and re-layouts  49.9 us (9%)
  loops' own time  45 us (8%)
  matrix products  25.2 us (4%)
  other arithmetic  21.3 us (4%)
  blocking collectives  20.1 us (3%)
  between operations  15.9 us (3%)
    reduce_scatter x1, waiting for transfers between devices, body(): lax.psum_scatter(seq_part, 'dp', scatter_dimension=0, tiled=True)  192 us
    all_gather x1, waiting for transfers between devices, body(): lax.all_gather(out_weight, ('seq', 'dp'), axis=0, tiled=True)  24.4 us
    all_to_all x1, waiting for transfers between devices, body(): lax.all_to_all(to_sources(back_q), 'dp', split_axis=0, concat_axis=0, til...  23.5 us
    all_to_all x1, waiting for transfers between devices, body(): lax.all_to_all(to_slots(q_rows), 'dp', split_axis=0, concat_axis=0, tiled...  22.5 us
    all_to_all x1, blocking collectives, body(): lax.all_to_all(to_sources(dv_tok), 'dp', split_axis=0, concat_axis=0, til...  20.1 us
  transfers between devices with their start and end apart: 17, of which 15 were waited for; matrix products, arithmetic and copies ran while one was open for 14% of the time, Pallas kernels for 0%

commit v1 on v0

--- a/solution.py
+++ b/solution.py
@@ -137,7 +137,12 @@
     tok_out = lax.all_to_all(head_out, "seq", split_axis=0, concat_axis=1, tiled=True)
     tok_grad = lax.dot_general(
         grad_tok,
-        lax.all_gather(out_weight, ("seq", "dp"), axis=0, tiled=True),
+        jnp.concatenate(
+            lax.all_to_all(
+                jnp.stack([out_weight] * lax.axis_size(("seq", "dp"))), ("seq", "dp"), 0, 0
+            ),
+            axis=0,
+        ),
         (((1,), (1,)), ((), ())),
         preferred_element_type=jnp.float32,
     ).astype(jnp.bfloat16)

time: 585 us -> 752 us (1.29)
  waiting for transfers between devices: 334 us -> 487 us
  blocking collectives: 20.1 us -> 30.9 us
    all_to_all x2, waiting for transfers between devices: 19.5 us -> 196 us  [the longest x1 186 us: body(): lax.all_to_all(jnp.stack([out_weight] * lax.axis_size(('seq', 'dp'))), ('...]
    all_gather x1 -> x0, waiting for transfers between devices: 24.4 us -> none  [body(): lax.all_gather(out_weight, ('seq', 'dp'), axis=0, tiled=True)]
    all_to_all x1 -> x2, blocking collectives: 20.1 us -> 30.9 us  [the longest x1 17.4 us: body(): lax.all_to_all(to_sources(dk_tok), 'dp', split_axis=0, concat_axis=0, til...]
  transfers between devices with their start and end apart: 17 -> 16, of which waited for: 15 -> 14; matrix products, arithmetic and copies ran while one was open for 14% -> 9% of each run, Pallas kernels for 0% -> 0%
where the time goes in v1:
time: 752 us; the launch traced here: 749 us
  waiting for transfers between devices  487 us (65%)
  starting transfers between devices  74.7 us (10%)
  local copies, waits for them, and re-layouts  51 us (7%)
  loops' own time  45.2 us (6%)
  blocking collectives  30.9 us (4%)
  matrix products  25.1 us (3%)
  other arithmetic  21.4 us (3%)
  between operations  14.5 us (2%)
    reduce_scatter x1, waiting for transfers between devices, body(): lax.psum_scatter(seq_part, 'dp', scatter_dimension=0, tiled=True)  192 us
    all_to_all x1, waiting for transfers between devices, body(): lax.all_to_all(jnp.stack([out_weight] * lax.axis_size(('seq', 'dp'))), ('...  186 us
    all_to_all x1, waiting for transfers between devices, body(): lax.all_to_all(to_sources(back_q), 'dp', split_axis=0, concat_axis=0, til...  23.3 us
    all_to_all x1, waiting for transfers between devices, body(): lax.all_to_all(to_slots(q_rows), 'dp', split_axis=0, concat_axis=0, tiled...  22.5 us
    all_to_all x1, blocking collectives, body(): lax.all_to_all(to_sources(dk_tok), 'dp', split_axis=0, concat_axis=0, til...  17.4 us
  transfers between devices with their start and end apart: 16, of which 14 were waited for; matrix products, arithmetic and copies ran while one was open for 9% of the time, Pallas kernels for 0%

profile of v1, /device:TPU:8, one launch (start us, length us, event | category | flops | bytes accessed | tf_op | source)
XLA Modules:
  0.0 749.3 jit_solution(4772899705749056468)
XLA Ops:
  10.8 11.3 %all-to-all-start = ((bf16[32,1,1]{2,1,0:T(2,128)(2,1)}), bf16[32,1,1]{2,1,0:T(2,128)(2,1)S(1)}, u32[]{:S(2)}, u32[]{:S(2)}) async-start(bf16[32,1,1]{2,1,0:T(2,128)(2,1)} %copy.81), calls=%async_computation | async-start | bytes 32768 | tf_op jit(solution)/shard_map/all_to_all | solution.py:43
  25.3 6.5 all-to-all-done
  39.3 8.4 %all-to-all-done.3 = bf16[32,8,512]{2,1,0:T(8,128)(2,1)S(1)} async-done(((bf16[32,8,512]{2,1,0:T(8,128)(2,1)}), bf16[32,8,512]{2,1,0:T(8,128)(2,1)S(1)}, u32[]{:S(2)}, u32[]{:S(2)}) %all-to-all-start.3) | async-done | bytes 262176 | tf_op jit(solution)/shard_map/all_to_all | solution.py:41
  54.6 22.5 %all-to-all-done.1 = bf16[32,8,2048]{2,1,0:T(8,128)(2,1)S(1)} async-done(((bf16[32,8,2048]{2,1,0:T(8,128)(2,1)}), bf16[32,8,2048]{2,1,0:T(8,128)(2,1)S(1)}, u32[]{:S(2)}, u32[]{:S(2)}) %all-to-all-start.1) | async-done | bytes 1048608 | tf_op jit(solution)/shard_map/all_to_all | solution.py:40
  87.0 6.9 all-to-all-done.7
  101.8 6.0 all-to-all-done.2
  124.9 22.9 %while.92 = (s32[]{:T(128)}, f32[2,2,512]{2,1,0:T(2,128)S(1)}, s32[2]{0:T(128)S(1)}, s32[2]{0:T(128)S(1)}, bf16[2,512,2,128]{3,1,2,0:T(8,128)(2,1)}, /*index=5*/...) while((s32[]{:T(128)}, f32[2,2,512]{2,1,0:T(2,128)S(1)}, ...), condition=%wide.region_12.13_spmd.clone.clone, body=%wide.region_7.12_spmd.clone.clone.sunk | while | flops 139202576 | bytes 5997160 | solution.py:109
  139.8 7.9 %while.97 = (s32[]{:T(128)}, f32[2,512]{1,0:T(2,128)S(1)}, f32[2,512]{1,0:T(2,128)S(1)}, s32[]{:T(128)}, s32[512]{0:T(512)S(1)}, /*index=5*/s32[1024]{0:T(1024)S...) while((s32[]{:T(128)}, f32[2,512]{1,0:T(2,128)S(1)}, ...), condition=%wide.region_11.11_spmd.clone, body=%wide.region_8.10_spmd.clone.sunk | while | flops 139201536 | bytes 5445827 | solution.py:103
  147.8 25.7 %while.94 = (s32[]{:T(128)}, bf16[2,512,256]{2,1,0:T(8,128)(2,1)S(1)}, s32[2]{0:T(128)S(1)}, s32[2]{0:T(128)S(1)}, bf16[2,512,2,128]{3,1,2,0:T(8,128)(2,1)}, /*i...) while((s32[]{:T(128)}, ...), condition=%wide.region_18.19_spmd.clone.clone, body=%wide.region_15.18_spmd.clone.clone.sunk | while | flops 272106496 | bytes 5543540 | solution.py:135
  164.2 8.8 %while.98 = (s32[]{:T(128)}, f32[2,512,128]{2,1,0:T(8,128)S(1)}, s32[]{:T(128)}, s32[512]{0:T(512)S(1)}, s32[1024]{0:T(1024)S(1)}, /*index=5*/s32[]{:T(128)}, s3...) while((s32[]{:T(128)}, f32[2,512,128]{2,1,0:T(8,128)S(1)}, ...), condition=%wide.region_17.17_spmd.clone, body=%wide.region_16.16_spmd.clone.sunk | while | flops 271975424 | bytes 2120903 | solution.py:125
  173.6 13.6 %all_to_all.181 = bf16[8,128,256]{2,1,0:T(8,128)(2,1)S(1)} all-to-all(bf16[8,128,256]{2,1,0:T(8,128)(2,1)S(1)} %bitcast.245), channel_id=1, replica_groups=mesh['seq'=8,'dp'=32] {'seq'}, dimensions={0} | all-to-all | bytes 1048576 | tf_op jit(solution)/shard_map/all_to_all | solution.py:137
  191.4 8.4 %all-to-all-start.5 = ((bf16[256,8,2048]{2,1,0:T(8,128)(2,1)}), bf16[256,8,2048]{2,1,0:T(8,128)(2,1)}, u32[]{:S(2)}, u32[]{:S(2)}) async-start(bf16[256,8,2048]{2,1,0:T(8,128)(2,1)} %stack.2), calls=%async_computation.5 | async-start | bytes 16777216 | tf_op jit(solution)/shard_map/all_to_all | solution.py:141
  201.1 185.7 %all-to-all-done.5 = bf16[256,8,2048]{2,1,0:T(8,128)(2,1)} async-done(((bf16[256,8,2048]{2,1,0:T(8,128)(2,1)}), bf16[256,8,2048]{2,1,0:T(8,128)(2,1)}, u32[]{:S(2)}, u32[]{:S(2)}) %all-to-all-start.5) | async-done | bytes 8388640 | tf_op jit(solution)/shard_map/all_to_all | solution.py:141
  386.8 6.3 fusion.55
  398.7 5.6 convolution_convert_fusion
  409.5 37.9 %while.96 = (s32[]{:T(128)}, f32[1024,128]{1,0:T(8,128)S(1)}, f32[1024,128]{1,0:T(8,128)S(1)}, bf16[2,512,256]{2,1,0:T(8,128)(2,1)}, s32[2]{0:T(128)S(1)}, /*ind...) while((s32[]{:T(128)}, f32[1024,128]{1,0:T(8,128)S(1)}, ...), condition=%wide.region_22.23_spmd.clone.clone, body=%wide.region_19.22_spmd.clone.clone.sunk | while | flops 677117952 | bytes 19322092 | solution.py:219
  418.1 6.3 while.99
  434.2 11.9 %while.99 = (s32[]{:T(128)}, f32[2,512,128]{2,1,0:T(8,128)S(1)}, f32[1024,128]{1,0:T(8,128)S(1)}, f32[1024,128]{1,0:T(8,128)S(1)}, s32[]{:T(128)}, /*index=5*/s3...) while((s32[]{:T(128)}, f32[2,512,128]{2,1,0:T(8,128)S(1)}, ...), condition=%wide.region_21.21_spmd.clone, body=%wide.region_20.20_spmd.clone.sunk | while | flops 676332544 | bytes 13527291 | solution.py:207
  463.8 6.1 all-to-all-done.13
  477.2 6.5 all-to-all-done.9
  483.6 17.4 %all_to_all.182 = bf16[32,8,512]{2,1,0:T(8,128)(2,1)S(1)} all-to-all(bf16[32,8,512]{2,1,0:T(8,128)(2,1)S(1)} %get-tuple-element.1149), channel_id=1, replica_groups=mesh['seq'=8,'dp'=32] {'dp'}, dimensions={0} | all-to-all | bytes 524288 | tf_op jit(solution)/shard_map/all_to_all | solution.py:250
  507.4 10.0 %all-to-all-done.14 = bf16[32,8,512]{2,1,0:T(8,128)(2,1)S(1)} async-done(((bf16[32,8,512]{2,1,0:T(8,128)(2,1)}), bf16[32,8,512]{2,1,0:T(8,128)(2,1)S(1)}, u32[]{:S(2)}, u32[]{:S(2)}) %all-to-all-start.14) | async-done | bytes 262176 | tf_op jit(solution)/shard_map/all_to_all | solution.py:251
  524.3 23.3 %all-to-all-done.10 = bf16[32,8,2048]{2,1,0:T(8,128)(2,1)S(1)} async-done(((bf16[32,8,2048]{2,1,0:T(8,128)(2,1)}), bf16[32,8,2048]{2,1,0:T(8,128)(2,1)S(1)}, u32[]{:S(2)}, u32[]{:S(2)}) %all-to-all-start.10) | async-done | bytes 1048608 | tf_op jit(solution)/shard_map/all_to_all | solution.py:249
  549.0 192.1 %reduce-scatter.5.cloned.1.call-done = bf16[8,2048]{1,0:T(8,128)(2,1)} async-done(((bf16[256,2048]{1,0:T(8,128)(2,1)}), bf16[8,2048]{1,0:T(8,128)(2,1)}) %reduce-scatter.5.cloned.1.call-update) | async-done | bytes 32784 | tf_op jit(solution)/shard_map/reduce_scatter | solution.py:160
  (246 shorter events, 162.2 us)
Async XLA Ops:
  7.2 379.6 %copy-start = (bf16[1,128,2048]{2,1,0:T(8,128)(2,1)S(1)}, bf16[1,128,2048]{2,1,0:T(8,128)(2,1)}, u32[]{:S(2)}) copy-start(bf16[1,128,2048]{2,1,0:T(8,128)(2,1)} %param.30) | copy-start | bytes 1572868
  7.2 29.6 %copy-start.2 = (bf16[128,2048]{1,0:T(8,128)(2,1)S(1)}, bf16[128,2048]{1,0:T(8,128)(2,1)}, u32[]{:S(2)}) copy-start(bf16[128,2048]{1,0:T(8,128)(2,1)} %param.24) | copy-start | bytes 1572868
  9.3 43.0 %copy-start.5 = (s32[16]{0:T(128)}, s32[16]{0:T(128)S(1)}, u32[]{:S(2)}) copy-start(s32[16]{0:T(128)S(1)} %get-tuple-element.1134) | copy-start | bytes 196
  10.8 21.0 %all-to-all-start = ((bf16[32,1,1]{2,1,0:T(2,128)(2,1)}), bf16[32,1,1]{2,1,0:T(2,128)(2,1)S(1)}, u32[]{:S(2)}, u32[]{:S(2)}) async-start(bf16[32,1,1]{2,1,0:T(2,128)(2,1)} %copy.81), calls=%async_computation | async-start | bytes 32768 | tf_op jit(solution)/shard_map/all_to_all | solution.py:43
  31.8 15.9 %all-to-all-start.3 = ((bf16[32,8,512]{2,1,0:T(8,128)(2,1)}), bf16[32,8,512]{2,1,0:T(8,128)(2,1)S(1)}, u32[]{:S(2)}, u32[]{:S(2)}) async-start(bf16[32,8,512]{2,1,0:T(8,128)(2,1)} %scatter_fusion.2), calls=%async_computation.3 | async-start | bytes 524288 | tf_op jit(solution)/shard_map/all_to_all | solution.py:41
  36.7 15.6 %copy-start.3 = (bf16[128,512]{1,0:T(8,128)(2,1)S(1)}, bf16[128,512]{1,0:T(8,128)(2,1)}, u32[]{:S(2)}) copy-start(bf16[128,512]{1,0:T(8,128)(2,1)} %param.26) | copy-start | bytes 393220
  47.7 29.4 %all-to-all-start.1 = ((bf16[32,8,2048]{2,1,0:T(8,128)(2,1)}), bf16[32,8,2048]{2,1,0:T(8,128)(2,1)S(1)}, u32[]{:S(2)}, u32[]{:S(2)}) async-start(bf16[32,8,2048]{2,1,0:T(8,128)(2,1)} %scatter_fusion), calls=%async_computation.1 | async-start | bytes 2097152 | tf_op jit(solution)/shard_map/all_to_all | solution.py:40
  77.1 16.9 %all-to-all-start.7 = ((bf16[32,8,512]{2,1,0:T(8,128)(2,1)}), bf16[32,8,512]{2,1,0:T(8,128)(2,1)S(1)}, u32[]{:S(2)}, u32[]{:S(2)}) async-start(bf16[32,8,512]{2,1,0:T(8,128)(2,1)} %scatter_fusion.4), calls=%async_computation.7 | async-start | bytes 524288 | tf_op jit(solution)/shard_map/all_to_all | solution.py:42
  93.9 13.8 %all-to-all-start.2 = ((bf16[128,8,256]{2,0,1:T(8,128)(2,1)}), bf16[128,8,256]{2,0,1:T(8,128)(2,1)S(1)}, u32[]{:S(2)}, u32[]{:S(2)}) async-start(bf16[128,8,256]{2,0,1:T(8,128)(2,1)} %copy.83), calls=%async_computation.2 | async-start | bytes 1048576 | tf_op jit(solution)/shard_map/all_to_all | solution.py:62
  108.5 10.9 %all-to-all-start.4 = ((bf16[128,8,128]{2,0,1:T(8,128)(2,1)}), bf16[128,8,128]{2,0,1:T(8,128)(2,1)S(1)}, u32[]{:S(2)}, u32[]{:S(2)}) async-start(bf16[128,8,128]{2,0,1:T(8,128)(2,1)} %bitcast.9), calls=%async_computation.4 | async-start | bytes 524288 | tf_op jit(solution)/shard_map/all_to_all | solution.py:63
  120.1 27.7 %all-to-all-start.8 = ((bf16[128,8,128]{2,0,1:T(8,128)(2,1)}), bf16[128,8,128]{2,0,1:T(8,128)(2,1)S(1)}, u32[]{:S(2)}, u32[]{:S(2)}) async-start(bf16[128,8,128]{2,0,1:T(8,128)(2,1)} %bitcast.17), calls=%async_computation.8 | async-start | bytes 524288 | tf_op jit(solution)/shard_map/all_to_all | solution.py:64
  147.8 39.3 %copy-start.4 = (bf16[8,2048]{1,0:T(8,128)(2,1)S(1)}, bf16[8,2048]{1,0:T(8,128)(2,1)}, u32[]{:S(2)}) copy-start(bf16[8,2048]{1,0:T(8,128)(2,1)} %param.31) | copy-start | bytes 98308
  191.4 195.3 %all-to-all-start.5 = ((bf16[256,8,2048]{2,1,0:T(8,128)(2,1)}), bf16[256,8,2048]{2,1,0:T(8,128)(2,1)}, u32[]{:S(2)}, u32[]{:S(2)}) async-start(bf16[256,8,2048]{2,1,0:T(8,128)(2,1)} %stack.2), calls=%async_computation.5 | async-start | bytes 16777216 | tf_op jit(solution)/shard_map/all_to_all | solution.py:141
  393.9 13.7 %all-to-all-start.6 = ((bf16[128,8,256]{2,0,1:T(8,128)(2,1)}), bf16[128,8,256]{2,0,1:T(8,128)(2,1)S(1)}, u32[]{:S(2)}, u32[]{:S(2)}) async-start(bf16[128,8,256]{2,0,1:T(8,128)(2,1)} %bitcast.167), calls=%async_computation.6 | async-start | bytes 1048576 | tf_op jit(solution)/shard_map/all_to_all | solution.py:158
  398.7 122.8 %reduce-scatter.3.cloned.1.call-start = ((), (), s32[]{:S(2)}) async-start(), calls=%async_computation.18 | async-start | bytes 9437184 | tf_op jit(solution)/shard_map/reduce_scatter | solution.py:150
  409.5 43.4 %copy-start.9 = (s32[32]{0:T(128)S(1)}, s32[32]{0:T(128)}, u32[]{:S(2)}) copy-start(s32[32]{0:T(128)} %get-tuple-element.1001) | copy-start | bytes 388
  448.1 10.9 %all-to-all-start.11 = ((bf16[8,128,128]{2,1,0:T(8,128)(2,1)}), bf16[8,128,128]{2,1,0:T(8,128)(2,1)S(1)}, u32[]{:S(2)}, u32[]{:S(2)}) async-start(bf16[8,128,128]{2,1,0:T(8,128)(2,1)} %bitcast.24), calls=%async_computation.11 | async-start | bytes 524288 | tf_op jit(solution)/shard_map/all_to_all | solution.py:225
  459.0 10.9 %all-to-all-start.13 = ((bf16[8,128,128]{2,1,0:T(8,128)(2,1)}), bf16[8,128,128]{2,1,0:T(8,128)(2,1)S(1)}, u32[]{:S(2)}, u32[]{:S(2)}) async-start(bf16[8,128,128]{2,1,0:T(8,128)(2,1)} %bitcast.28), calls=%async_computation.13 | async-start | bytes 524288 | tf_op jit(solution)/shard_map/all_to_all | solution.py:226
  469.9 13.8 %all-to-all-start.9 = ((bf16[8,128,256]{2,1,0:T(8,128)(2,1)}), bf16[8,128,256]{2,1,0:T(8,128)(2,1)S(1)}, u32[]{:S(2)}, u32[]{:S(2)}) async-start(bf16[8,128,256]{2,1,0:T(8,128)(2,1)} %bitcast.20), calls=%async_computation.9 | async-start | bytes 1048576 | tf_op jit(solution)/shard_map/all_to_all | solution.py:224
  474.9 30.2 %copy-start.8 = (s32[32]{0:T(128)S(1)}, s32[32]{0:T(128)}, u32[]{:S(2)}) copy-start(s32[32]{0:T(128)} %get-tuple-element.1150) | copy-start | bytes 388
  501.0 16.4 %all-to-all-start.14 = ((bf16[32,8,512]{2,1,0:T(8,128)(2,1)}), bf16[32,8,512]{2,1,0:T(8,128)(2,1)S(1)}, u32[]{:S(2)}, u32[]{:S(2)}) async-start(bf16[32,8,512]{2,1,0:T(8,128)(2,1)} %get-tuple-element.1148), calls=%async_computation.14 | async-start | bytes 524288 | tf_op jit(solution)/shard_map/all_to_all | solution.py:251
  507.4 14.9 %copy-start.6 = (s32[16]{0:T(128)S(1)}, s32[16]{0:T(128)}, u32[]{:S(2)}) copy-start(s32[16]{0:T(128)} %copy-done.5) | copy-start | bytes 196
  517.5 30.1 %all-to-all-start.10 = ((bf16[32,8,2048]{2,1,0:T(8,128)(2,1)}), bf16[32,8,2048]{2,1,0:T(8,128)(2,1)S(1)}, u32[]{:S(2)}, u32[]{:S(2)}) async-start(bf16[32,8,2048]{2,1,0:T(8,128)(2,1)} %broadcast_select_fusion), calls=%async_computation.10 | async-start | bytes 2097152 | tf_op jit(solution)/shard_map/all_to_all | solution.py:249
  521.4 219.7 %reduce-scatter.5.cloned.1.call-start = ((), (), s32[]{:S(2)}) async-start(), calls=%async_computation.19 | async-start | bytes 1081344 | tf_op jit(solution)/shard_map/reduce_scatter | solution.py:160
  (2 other events, 28.1 us)
Sparse Core Ops, SparseCore 0:
  404.4 48.0 reduce-scatter.2
  526.1 215.0 reduce-scatter.4
